TPU v7x, 256 devices: a whole 4x4x8 slice. The times are simulated.
256 devices in a mesh: row: 64 (over z, y, x_hi), col: 2 (over core), layer: 2 (over x_lo).
Axes of the slice: x: 4 (x_hi: 2, x_lo: 2; x = x_hi * 2 + x_lo), y: 4, z: 8, core: 2. Of those that a mesh axis runs over, the one named last changes fastest.
Arguments:
- a_blocks: bfloat16 [64, 128, 64, 64], P('row', ('col', 'layer')), may hold values from -6 to 6
- a_index: int32 [64, 128, 2], P('row', ('col', 'layer')), may hold values from 0 to 511, as said below
- a_count: int32 [64, 4], P('row', ('col', 'layer')), may hold values from 1 to 32, as said below
- b_blocks: bfloat16 [512, 2, 64, 64], P(('row', 'layer'), 'col'), may hold values from -0.75 to 0.75
- b_index: int32 [512, 2, 2], P(('row', 'layer'), 'col'), may hold values from 0 to 15, as said below
- b_count: int32 [128, 2], P(('row', 'layer'), 'col'), may hold values from 1 to 4, as said below
Outputs:
- product: bfloat16 [32768, 1024], P(('row', 'layer'), 'col')
Inputs may be any that keep to these rules, and one draw needn't show every extreme that they name: `a_index`: within one piece the live slots name distinct (block row, inner block) positions; entry 0 is below 8, entry 1 below 512. `b_index`: within one piece the live slots name distinct (inner block, block column) positions; entry 0 is below 16, entry 1 below 8. `a_count`: some piece is full. `b_count`: some piece is full.
All inputs are finite; a program needn't handle non-finite values.
Results may differ from a plain program's by a relative error of at most 0.001.
Values may be sent and summed in bfloat16 or wider, within the bound.
No kernel may reach another device: no remote copies, remote signals or barrier semaphores. Data moves between devices by JAX's collectives and lax.ppermute only.
A program may use at most 128 MiB of HBM per device.

v0:
```python
import math
import jax
import jax.numpy as jnp
from jax import lax
from jax.sharding import PartitionSpec as P

BLK = 64
NB = 2048
RW = 8
KW = 8


def tile_product(a_vals, a_rows, a_keys, b_vals, b_keys, b_cols, row_count, col_count):
    count = b_vals.shape[0]
    hit = (a_keys[:, None, None] == b_keys[None, None, :]) & (
        b_cols[None, None, :] == jnp.arange(col_count, dtype=jnp.int32)[None, :, None]
    )
    chosen = jnp.sum(jnp.where(hit, jnp.arange(count, dtype=jnp.int32)[None, None, :], 0), axis=2)
    found = jnp.any(hit, axis=2)
    picked = b_vals[chosen] * found[:, :, None, None].astype(b_vals.dtype)
    terms = jnp.einsum("axy,ajyz->axjz", a_vals, picked, preferred_element_type=jnp.float32)
    place = (a_rows[:, None] == jnp.arange(row_count, dtype=jnp.int32)[None, :]).astype(jnp.float32)
    summed = jnp.dot(place.T, terms.reshape(terms.shape[0], -1), precision=lax.Precision.HIGHEST)
    return summed.reshape(row_count * BLK, col_count * BLK)


def on_device(a_blocks, a_index, a_count, b_blocks, b_index, b_count):
    slots_a = a_blocks.shape[1]
    slots_b = b_blocks.shape[0]
    layers = lax.axis_size("layer")
    inner_a = NB // (layers * lax.axis_size("col"))
    inner_b = NB // (layers * lax.axis_size("row"))
    a_keys = jnp.where(jnp.arange(slots_a, dtype=jnp.int32) < a_count[0, 0], a_index[0, :, 1], -1)[
        None, :
    ]
    a_rows = a_index[0, :, 0][None, :]
    b_keys = jnp.where(jnp.arange(slots_b, dtype=jnp.int32) < b_count[0, 0], b_index[:, 0, 0], -1)[
        :, None
    ]
    b_cols = b_index[:, 0, 1][:, None]
    b_vals, b_raw, b_col_all = (
        lax.all_gather(b_blocks, "row", axis=0, tiled=True),
        lax.all_gather(b_keys, "row", axis=0, tiled=True),
        lax.all_gather(b_cols, "row", axis=0, tiled=True),
    )
    piece_b = jnp.arange(b_raw.shape[0], dtype=jnp.int32) // slots_b
    b_glob = jnp.where(b_raw[:, 0] >= 0, piece_b * inner_b + b_raw[:, 0], -2).astype(jnp.int32)
    row_count = RW
    b_flat = b_vals[:, 0]
    b_col_flat = b_col_all[:, 0]
    empty = jnp.zeros((row_count * BLK, KW * BLK), jnp.float32)

    def fold_rows(total, vals, rows, glob):
        taken = glob.shape[0]
        step = slots_a * math.gcd(taken // slots_a, 8)
        turns = taken // step

        def one_turn(index, acc):
            return acc + tile_product(vals, rows, glob, b_flat, b_glob, b_col_flat, row_count, KW)

        return lax.fori_loop(0, turns, one_turn, total)

    vals = lax.all_gather(a_blocks, "col", axis=1, tiled=True)
    keys = lax.all_gather(a_keys, "col", axis=1, tiled=True)
    rows = lax.all_gather(a_rows, "col", axis=1, tiled=True)
    taken = keys.shape[1]
    group = jnp.arange(taken, dtype=jnp.int32) // slots_a
    glob = jnp.where(keys[0] >= 0, group * inner_a + keys[0], -1).astype(jnp.int32)
    partial_tile = fold_rows(empty, vals[0], rows[0], glob)
    return lax.psum_scatter(partial_tile, "layer", scatter_dimension=0, tiled=True).astype(
        jnp.bfloat16
    )


def solution(mesh):
    in_specs = (
        P("row", ("col", "layer"), None, None),
        P("row", ("col", "layer"), None),
        P("row", ("col", "layer")),
        P(("row", "layer"), "col", None, None),
        P(("row", "layer"), "col", None),
        P(("row", "layer"), "col"),
    )
    out_specs = P(("row", "layer"), "col")
    return jax.shard_map(
        on_device, mesh=mesh, in_specs=in_specs, out_specs=out_specs, check_vma=False
    )
```

profile of v0, /device:TPU:1, one launch (start us, length us, event | category | flops | bytes accessed | tf_op | source)
XLA Modules:
  0.0 255.7 jit_solution(8151125068441532517)
XLA Ops:
  6.5 0.7 all-gather.4.cloned.1.call-update
  8.6 1.3 dynamic-slice.2
  9.9 1.3 dynamic-slice
  12.4 0.8 bitcast_dynamic-update-slice_fusion.1
  13.2 0.8 fusion.11
  14.0 4.7 %all-reduce.5 = (s32[64]{0:T(128)S(1)}, s32[64]{0:T(128)S(1)}) all-reduce(s32[64]{0:T(128)S(1)} %fusion.11, s32[64]{0:T(128)S(1)} %bitcast_dynamic-update-slice_fusion.1), channel_id=1, replica_groups=mesh['row'=64,'col'=2,'layer'=2] {'col'}, use_global_device_ids=true, to_apply=%add.1 | all-reduce | flops 128 | bytes 1024 | tf_op jit(solution)/shard_map/squeeze | solution.py:68
  18.7 0.8 bitcast_dynamic-update-slice_fusion
  19.5 0.8 fusion.13
  20.2 21.5 %all-reduce.4 = (s32[256]{0:T(256)S(1)}, s32[256]{0:T(256)S(1)}) all-reduce(s32[256]{0:T(256)S(1)} %bitcast_dynamic-update-slice_fusion, s32[256]{0:T(256)S(1)} %fusion.13), channel_id=3, replica_groups=mesh['row'=64,'col'=2,'layer'=2] {'row'}, use_global_device_ids=true, to_apply=%add.3 | all-reduce | flops 512 | bytes 4096
  41.7 0.1 broadcast_compare_fusion
  41.8 1.2 and_reduce_fusion
  43.0 1.2 fusion.3
  44.2 0.1 reshape.170
  44.3 7.5 %all_gather.23 = bf16[1,64,64,64]{3,2,0,1:T(8,128)(2,1)S(1)} all-gather(bf16[1,32,64,64]{3,2,0,1:T(8,128)(2,1)} %bitcast.42), channel_id=1, replica_groups=mesh['row'=64,'col'=2,'layer'=2] {'col'}, dimensions={1}, use_global_device_ids=true | all-gather | bytes 786432 | tf_op jit(solution)/shard_map/all_gather | solution.py:63
  51.8 87.9 %all-gather.4.cloned.1.call-done = bf16[256,1,64,64]{3,2,1,0:T(8,128)(2,1)} async-done(((bf16[4,1,64,64]{3,2,1,0:T(8,128)(2,1)}), bf16[256,1,64,64]{3,2,1,0:T(8,128)(2,1)}) %all-gather.4.cloned.1.call-update) | async-done | bytes 2097168 | tf_op jit(solution)/shard_map/all_gather | solution.py:42
  139.6 21.7 %gather_fusion = bf16[512,64,64]{2,1,0:T(8,128)(2,1)} fusion(bf16[256,64,64]{2,1,0:T(8,128)(2,1)} %bitcast.41, s32[1024]{0:T(1024)S(1)} %pad_clamp_fusion), kind=kCustom, calls=%fused_computation | custom fusion | bytes 8390656 | tf_op jit(solution)/shard_map/while/body/eval_jaxpr/gather | solution.py:20
  161.4 11.9 %copy.13 = bf16[64,8,64,64]{2,3,1,0:T(8,128)(2,1)} copy(bf16[64,8,64,64]{3,2,1,0:T(8,128)(2,1)} %bitcast.40) | data formatting | bytes 8388608 | tf_op jit(solution)/shard_map/while/body/eval_jaxpr/gather | solution.py:20
  173.3 11.5 %convolution_bitcast_fusion = f32[64,64,8,64]{1,3,2,0:T(8,128)} fusion(bf16[64,8,64,64]{2,3,1,0:T(8,128)(2,1)} %copy.13, bf16[64,8]{1,0:T(8,128)(2,1)S(1)} %convert_element_type.14, bf16[1,64,64,64]{3,2,0,1:T(8,128)(2,1)S(1)} %all_gather.23), kind=kOutput, calls=%fused_computation.1 | convolution fusion | flops 270532608 | bytes 13108224 | tf_op jit(solution)/shard_map/while/body/eval_jaxpr/axy,ajyz->axjz/dot_general | solution.py:21
  184.8 17.5 %copy.15 = f32[64,64,8,64]{3,2,1,0:T(8,128)} copy(f32[64,64,8,64]{1,3,2,0:T(8,128)} %convolution_bitcast_fusion) | data formatting | bytes 16777216 | tf_op jit(solution)/shard_map/while/body/eval_jaxpr/axy,ajyz->axjz/dot_general | solution.py:21
  202.2 12.9 %reshape.166 = f32[64,32768]{1,0:T(8,128)} reshape(f32[64,64,8,64]{3,2,1,0:T(8,128)} %copy.15) | data formatting | bytes 16777216 | tf_op jit(solution)/shard_map/while/body/eval_jaxpr/reshape | solution.py:23
  215.1 5.2 %fusion.4 = f32[8,32768]{1,0:T(8,128)S(1)} fusion(f32[64,32768]{1,0:T(8,128)} %reshape.166, s32[64]{0:T(128)S(1)} %get-tuple-element.22), kind=kOutput, calls=%fused_computation.11 | convolution fusion | flops 201327104 | bytes 9437440 | tf_op jit(solution)/shard_map/while/body/eval_jaxpr/dot_general | solution.py:23
  220.3 1.2 reshape.167
  221.5 25.6 %reduce-scatter.2.cloned.1.call-done = f32[256,512]{1,0:T(8,128)} async-done(((f32[512,512]{1,0:T(8,128)}), f32[256,512]{1,0:T(8,128)}) %reduce-scatter.2.cloned.1.call-update) | async-done | bytes 524304 | tf_op jit(solution)/shard_map/reduce_scatter | solution.py:70
  247.1 1.8 convert_element_type.15
  (13 shorter events, 0.1 us)
Async XLA Ops:
  6.5 133.1 %all-gather.4.cloned.1.call-start = ((), (), s32[]{:S(2)}) async-start(), calls=%async_computation.1 | async-start | bytes 4259840 | tf_op jit(solution)/shard_map/all_gather | solution.py:42
  7.3 239.8 %reduce-scatter.2.cloned.1.call-start = ((), (), s32[]{:S(2)}) async-start(), calls=%async_computation.2 | async-start | bytes 1572864 | tf_op jit(solution)/shard_map/reduce_scatter | solution.py:70
Sparse Core Ops, SparseCore 0:
  11.1 128.4 all-gather.3
  221.6 25.4 reduce-scatter.1
where the time goes:
time: 257 us; the launch traced here: 256 us
  waiting for transfers between devices  114 us (44%)
  local copies, waits for them, and re-layouts  69.4 us (27%)
  blocking collectives  33.6 us (13%)
  matrix products  16.7 us (6%)
  between operations  16 us (6%)
  other arithmetic  5.76 us (2%)
    all_gather x1, waiting for transfers between devices, on_device(): lax.all_gather(b_blocks, 'row', axis=0, tiled=True)  87.9 us
    gather x2, local copies, waits for them, and re-layouts, tile_product(): picked = b_vals[chosen] * found[:, :, None, None].astype(b_vals.dtype)  33.7 us
    reduce_scatter x1, waiting for transfers between devices, on_device(): lax.psum_scatter(partial_tile, 'layer', scatter_dimension=0, tiled=True)  25.6 us
    unnamed x1, blocking collectives  21.5 us
    dot_general x1, local copies, waits for them, and re-layouts, tile_product(): jnp.einsum('axy,ajyz->axjz', a_vals, picked, preferred_element_type=jnp.f...  17.5 us
    reshape x1, local copies, waits for them, and re-layouts, tile_product(): terms.reshape(terms.shape[0], -1)  12.9 us
    dot_general x1, matrix products, tile_product(): jnp.einsum('axy,ajyz->axjz', a_vals, picked, preferred_element_type=jnp.f...  11.5 us
    all_gather x1, blocking collectives, on_device(): vals = lax.all_gather(a_blocks, 'col', axis=1, tiled=True)  7.45 us
  transfers between devices with their start and end apart: 2, of which 2 were waited for; matrix products, arithmetic and copies ran while one was open for 3% of the time, Pallas kernels for 0%

commit v1 on v0

--- a/solution.py
+++ b/solution.py
@@ -39,7 +39,9 @@
     ]
     b_cols = b_index[:, 0, 1][:, None]
     b_vals, b_raw, b_col_all = (
-        lax.all_gather(b_blocks, "row", axis=0, tiled=True),
+        jnp.concatenate(
+            lax.all_to_all(jnp.stack([b_blocks] * lax.axis_size("row")), "row", 0, 0), axis=0
+        ),
         lax.all_gather(b_keys, "row", axis=0, tiled=True),
         lax.all_gather(b_cols, "row", axis=0, tiled=True),
     )

time: 257 us -> 214 us (0.83)
  waiting for transfers between devices: 114 us -> 24.8 us
  blocking collectives: 33.6 us -> 53.4 us
  starting transfers between devices: 0.04 us -> 15.2 us
  local copies, waits for them, and re-layouts: 69.4 us -> 82.2 us
    all_gather x1 -> x0, waiting for transfers between devices: 87.9 us -> none  [on_device(): lax.all_gather(b_blocks, 'row', axis=0, tiled=True)]
    unnamed x1, blocking collectives: 21.5 us -> 46.5 us
    all_to_all x0 -> x1, starting transfers between devices: none -> 15.1 us  [on_device(): lax.all_to_all(jnp.stack([b_blocks] * lax.axis_size('row')), 'row', 0, 0)]
    unnamed x8 -> x23, local copies, waits for them, and re-layouts: 4.1 us -> 17.1 us
    all_gather x1, blocking collectives: 7.45 us -> 4.44 us  [on_device(): vals = lax.all_gather(a_blocks, 'col', axis=1, tiled=True)]
  transfers between devices with their start and end apart: 2 -> 2, of which waited for: 2 -> 1; matrix products, arithmetic and copies ran while one was open for 3% -> 2% of each run, Pallas kernels for 0% -> 0%
where the time goes in v1:
time: 214 us; the launch traced here: 213 us
  local copies, waits for them, and re-layouts  82.2 us (38%)
  blocking collectives  53.4 us (25%)
  waiting for transfers between devices  24.8 us (12%)
  matrix products  16.7 us (8%)
  between operations  16.1 us (8%)
  starting transfers between devices  15.2 us (7%)
  other arithmetic  4.41 us (2%)
    unnamed x1, blocking collectives  46.5 us
    gather x2, local copies, waits for them, and re-layouts, tile_product(): picked = b_vals[chosen] * found[:, :, None, None].astype(b_vals.dtype)  33.5 us
    reduce_scatter x1, waiting for transfers between devices, on_device(): lax.psum_scatter(partial_tile, 'layer', scatter_dimension=0, tiled=True)  24.8 us
    dot_general x1, local copies, waits for them, and re-layouts, tile_product(): jnp.einsum('axy,ajyz->axjz', a_vals, picked, preferred_element_type=jnp.f...  17.5 us
    unnamed x23, local copies, waits for them, and re-layouts  17.1 us
    all_to_all x1, starting transfers between devices, on_device(): lax.all_to_all(jnp.stack([b_blocks] * lax.axis_size('row')), 'row', 0, 0)  15.1 us
    reshape x1, local copies, waits for them, and re-layouts, tile_product(): terms.reshape(terms.shape[0], -1)  12.9 us
    dot_general x1, matrix products, tile_product(): jnp.einsum('axy,ajyz->axjz', a_vals, picked, preferred_element_type=jnp.f...  11.5 us
  transfers between devices with their start and end apart: 2, of which 1 were waited for; matrix products, arithmetic and copies ran while one was open for 2% of the time, Pallas kernels for 0%

profile of v1, /device:TPU:1, one launch (start us, length us, event | category | flops | bytes accessed | tf_op | source)
XLA Modules:
  0.0 212.8 jit_solution(14727403905578967136)
XLA Ops:
  6.5 0.8 copy-done
  7.4 3.0 %broadcast_bitcast_fusion = bf16[64,1,4,64,64]{4,3,2,1,0:T(8,128)(2,1)} fusion(bf16[4,64,64]{2,1,0:T(8,128)(2,1)S(1)} %bitcast.44), kind=kLoop, calls=%fused_computation.37 | loop fusion | bytes 2129920
  10.4 7.9 %reshape.209 = bf16[64,2,8192]{2,1,0:T(2,128)(2,1)} reshape(bf16[64,1,4,64,64]{4,3,2,1,0:T(8,128)(2,1)} %broadcast_bitcast_fusion) | data formatting | bytes 4194304
  18.2 15.1 %all-to-all-start = ((bf16[64,2,8192]{2,1,0:T(2,128)(2,1)}), bf16[64,2,8192]{2,1,0:T(2,128)(2,1)S(1)}, u32[]{:S(2)}, u32[]{:S(2)}) async-start(bf16[64,2,8192]{2,1,0:T(2,128)(2,1)} %reshape.209), calls=%async_computation | async-start | bytes 4194304 | tf_op jit(solution)/shard_map/all_to_all | solution.py:43
  34.7 0.6 dynamic-slice.2
  35.3 0.6 dynamic-slice
  37.2 0.1 bitcast_dynamic-update-slice_fusion.1
  37.3 0.1 fusion.11
  37.4 2.4 %all-reduce.5 = (s32[64]{0:T(128)S(1)}, s32[64]{0:T(128)S(1)}) all-reduce(s32[64]{0:T(128)S(1)} %fusion.11, s32[64]{0:T(128)S(1)} %bitcast_dynamic-update-slice_fusion.1), channel_id=1, replica_groups=mesh['row'=64,'col'=2,'layer'=2] {'col'}, use_global_device_ids=true, to_apply=%add.1 | all-reduce | flops 128 | bytes 1024 | tf_op jit(solution)/shard_map/squeeze | solution.py:70
  39.9 0.1 fusion.13
  40.0 46.5 %all-reduce.4 = (s32[256]{0:T(256)S(1)}, s32[256]{0:T(256)S(1)}) all-reduce(s32[256]{0:T(256)S(1)} %bitcast_dynamic-update-slice_fusion, s32[256]{0:T(256)S(1)} %fusion.13), channel_id=3, replica_groups=mesh['row'=64,'col'=2,'layer'=2] {'row'}, use_global_device_ids=true, to_apply=%add.3 | all-reduce | flops 512 | bytes 4096
  86.7 1.2 and_reduce_fusion
  87.9 1.2 fusion.3
  89.2 4.4 %all_gather.19 = bf16[1,64,64,64]{3,2,0,1:T(8,128)(2,1)S(1)} all-gather(bf16[1,32,64,64]{3,2,0,1:T(8,128)(2,1)} %bitcast.47), channel_id=1, replica_groups=mesh['row'=64,'col'=2,'layer'=2] {'col'}, dimensions={1}, use_global_device_ids=true | all-gather | bytes 786432 | tf_op jit(solution)/shard_map/all_gather | solution.py:65
  93.6 4.0 %reshape.210 = bf16[64,1,4,64,64]{4,3,2,1,0:T(8,128)(2,1)} reshape(bf16[64,2,8192]{2,1,0:T(2,128)(2,1)S(1)} %all-to-all-done) | data formatting | bytes 4194304
  97.6 21.6 %gather_fusion = bf16[512,64,64]{2,1,0:T(8,128)(2,1)} fusion(bf16[256,64,64]{2,1,0:T(8,128)(2,1)} %bitcast.45, s32[1024]{0:T(1024)S(1)} %pad_clamp_fusion), kind=kCustom, calls=%fused_computation | custom fusion | bytes 8390656 | tf_op jit(solution)/shard_map/while/body/eval_jaxpr/gather | solution.py:20
  119.2 11.9 %copy.12 = bf16[64,8,64,64]{2,3,1,0:T(8,128)(2,1)} copy(bf16[64,8,64,64]{3,2,1,0:T(8,128)(2,1)} %bitcast.46) | data formatting | bytes 8388608 | tf_op jit(solution)/shard_map/while/body/eval_jaxpr/gather | solution.py:20
  131.1 11.5 %convolution_bitcast_fusion = f32[64,64,8,64]{1,3,2,0:T(8,128)} fusion(bf16[64,8,64,64]{2,3,1,0:T(8,128)(2,1)} %copy.12, bf16[64,8]{1,0:T(8,128)(2,1)S(1)} %convert_element_type.14, bf16[1,64,64,64]{3,2,0,1:T(8,128)(2,1)S(1)} %all_gather.19), kind=kOutput, calls=%fused_computation.1 | convolution fusion | flops 270532608 | bytes 13108224 | tf_op jit(solution)/shard_map/while/body/eval_jaxpr/axy,ajyz->axjz/dot_general | solution.py:21
  142.6 17.5 %copy.14 = f32[64,64,8,64]{3,2,1,0:T(8,128)} copy(f32[64,64,8,64]{1,3,2,0:T(8,128)} %convolution_bitcast_fusion) | data formatting | bytes 16777216 | tf_op jit(solution)/shard_map/while/body/eval_jaxpr/axy,ajyz->axjz/dot_general | solution.py:21
  160.1 12.9 %reshape.169 = f32[64,32768]{1,0:T(8,128)} reshape(f32[64,64,8,64]{3,2,1,0:T(8,128)} %copy.14) | data formatting | bytes 16777216 | tf_op jit(solution)/shard_map/while/body/eval_jaxpr/reshape | solution.py:23
  173.0 5.2 %fusion.4 = f32[8,32768]{1,0:T(8,128)S(1)} fusion(f32[64,32768]{1,0:T(8,128)} %reshape.169, s32[64]{0:T(128)S(1)} %get-tuple-element.22), kind=kOutput, calls=%fused_computation.11 | convolution fusion | flops 201327104 | bytes 9437440 | tf_op jit(solution)/shard_map/while/body/eval_jaxpr/dot_general | solution.py:23
  178.2 1.2 reshape.170
  179.4 24.8 %reduce-scatter.2.cloned.1.call-done = f32[256,512]{1,0:T(8,128)} async-done(((f32[512,512]{1,0:T(8,128)}), f32[256,512]{1,0:T(8,128)}) %reduce-scatter.2.cloned.1.call-update) | async-done | bytes 524304 | tf_op jit(solution)/shard_map/reduce_scatter | solution.py:72
  204.2 1.8 convert_element_type.15
  (27 shorter events, 0.4 us)
Async XLA Ops:
  6.5 0.8 copy-start
  6.5 28.2 %copy-start.5 = (u32[256]{0:T(256)S(1)}, u32[256]{0:T(256)}, u32[]{:S(2)}) copy-start(u32[256]{0:T(256)} %constant.74) | copy-start | bytes 3076
  6.5 28.8 %copy-start.4 = (u32[256]{0:T(256)S(1)}, u32[256]{0:T(256)}, u32[]{:S(2)}) copy-start(u32[256]{0:T(256)} %constant.64) | copy-start | bytes 3076
  6.5 30.7 %copy-start.2 = (s32[1,32,2]{1,2,0:T(2,128)S(1)}, s32[1,32,2]{1,2,0:T(2,128)}, u32[]{:S(2)}) copy-start(s32[1,32,2]{1,2,0:T(2,128)} %param.7) | copy-start | bytes 772
  6.5 33.3 %copy-start.3 = (s32[4,1,2]{0,2,1:T(2,128)S(1)}, s32[4,1,2]{0,2,1:T(2,128)}, u32[]{:S(2)}) copy-start(s32[4,1,2]{0,2,1:T(2,128)} %param.10) | copy-start | bytes 100
  18.2 75.4 %all-to-all-start = ((bf16[64,2,8192]{2,1,0:T(2,128)(2,1)}), bf16[64,2,8192]{2,1,0:T(2,128)(2,1)S(1)}, u32[]{:S(2)}, u32[]{:S(2)}) async-start(bf16[64,2,8192]{2,1,0:T(2,128)(2,1)} %reshape.209), calls=%async_computation | async-start | bytes 4194304 | tf_op jit(solution)/shard_map/all_to_all | solution.py:43
  33.4 170.8 %reduce-scatter.2.cloned.1.call-start = ((), (), s32[]{:S(2)}) async-start(), calls=%async_computation.2 | async-start | bytes 1572864 | tf_op jit(solution)/shard_map/reduce_scatter | solution.py:72
  160.1 45.9 %copy-start.1 = (bf16[4,1,64,64]{3,2,1,0:T(8,128)(2,1)S(1)}, bf16[4,1,64,64]{3,2,1,0:T(8,128)(2,1)}, u32[]{:S(2)}) copy-start(bf16[4,1,64,64]{3,2,1,0:T(8,128)(2,1)} %param.9) | copy-start | bytes 98308
Sparse Core Ops, SparseCore 0:
  179.5 24.6 reduce-scatter.1
